TPU v7x, 32 devices: a whole 2x2x4 slice. The times are simulated.
32 devices in a mesh: seq: 8 (over z, x), feat: 4 (over y, core).
Axes of the slice: x: 2, y: 2, z: 4, core: 2. Of those that a mesh axis runs over, the one named last changes fastest.
Arguments:
- tokens: bfloat16 [8192, 4096], P('seq', 'feat'), may hold values from -18 to 18
- segment_ids: int32 [8192], P('seq'), may hold values from 0 to 5, never falling along the last dimension, each value on 1 to 4096 neighbouring positions
- q_weight: bfloat16 [4096, 4096], P('seq', 'feat'), may hold values from -0.09375 to 0.09375
- k_weight: bfloat16 [4096, 1024], P('seq'), may hold values from -0.09375 to 0.09375
- v_weight: bfloat16 [4096, 1024], P('seq'), may hold values from -0.09375 to 0.09375
- o_weight: bfloat16 [4096, 4096], P('seq', 'feat'), may hold values from -0.09375 to 0.09375
Outputs:
- attention_out: bfloat16 [8192, 4096], P('seq', 'feat')
Inputs may be any that keep to these rules, and one draw needn't show every extreme that they name: `segment_ids`: document numbers never fall along the window; each document is 1 to 4096 positions long and one is exactly that long.
All inputs are finite; a program needn't handle non-finite values.
Results may differ from a plain program's by a relative error of at most 0.011.
Values may be sent and summed in bfloat16 or wider, within the bound.
A program may use at most 192 MiB of HBM per device.

v0:
```python
import math

import jax
import jax.numpy as jnp
from jax import lax
from jax.sharding import PartitionSpec as P

H = 32
KVH = 8
HD = 128
KVD = 1024


rope_base = 500000.0


def rotary(matrix, positions):
    columns = matrix.shape[1]
    pair_index = (jnp.arange(columns // 2, dtype=jnp.int32) % (HD // 2)).astype(jnp.float32)
    frequency = jnp.exp(-(2.0 * pair_index / HD) * math.log(rope_base))
    angle = positions.astype(jnp.float32)[:, None] * frequency[None, :]
    cosine = jnp.cos(angle)
    sine = jnp.sin(angle)
    paired = matrix.reshape(matrix.shape[0], columns // 2, 2)
    first = paired[..., 0]
    second = paired[..., 1]
    turned = jnp.stack([first * cosine - second * sine, first * sine + second * cosine], -1)
    return turned.reshape(matrix.shape)


def attend_block(state, block_keys, block_values, block_segments, key_start, context):
    queries, query_segments, query_start, kv_heads = context
    running_max, running_sum, weighted = state
    query_count = queries.shape[0]
    key_count = block_keys.shape[0]
    query_heads = queries.reshape(query_count, kv_heads, -1, HD)
    key_heads = block_keys.reshape(key_count, kv_heads, HD)
    value_heads = block_values.reshape(key_count, kv_heads, HD)
    scores = jnp.einsum(
        "rngd,knd->ngrk", query_heads, key_heads, preferred_element_type=jnp.float32
    ) * (1.0 / math.sqrt(HD))
    query_positions = query_start + jnp.arange(query_count, dtype=jnp.int32)
    key_positions = key_start + jnp.arange(key_count, dtype=jnp.int32)
    allowed = (key_positions[None, :] <= query_positions[:, None]) & (
        block_segments[None, :] == query_segments[:, None]
    )
    scores = jnp.where(allowed, scores, -1e30)
    new_max = jnp.maximum(running_max, jnp.max(scores, axis=-1))
    probs = jnp.where(allowed, jnp.exp(scores - new_max[..., None]), 0.0)
    rescale = jnp.exp(running_max - new_max)
    new_sum = running_sum * rescale + jnp.sum(probs, axis=-1)
    new_weighted = weighted * rescale[..., None] + jnp.einsum(
        "ngrk,knd->ngrd",
        probs.astype(jnp.bfloat16),
        value_heads,
        preferred_element_type=jnp.float32,
    )
    return (new_max, new_sum, new_weighted)


def fold_piece(state, piece, context):
    piece_keys, piece_values, piece_segments = piece
    key_total = piece_keys.shape[0]
    block_width = 1024
    block_count = key_total // block_width
    last_query = context[2] + context[0].shape[0] - 1

    def one_block(number, carried):
        begin = number * block_width
        block_keys = lax.dynamic_slice_in_dim(piece_keys, begin, block_width, 0)
        block_values = lax.dynamic_slice_in_dim(piece_values, begin, block_width, 0)
        block_segments = lax.dynamic_slice_in_dim(piece_segments, begin, block_width, 0)
        return lax.cond(
            begin <= last_query,
            lambda inner: attend_block(
                inner, block_keys, block_values, block_segments, begin, context
            ),
            lambda inner: inner,
            carried,
        )

    return lax.fori_loop(0, block_count, one_block, state)


def local(tokens, segment_ids, q_weight, k_weight, v_weight, o_weight):
    feat_count = lax.axis_size("feat")
    feat_index = lax.axis_index("feat")
    head_count = q_weight.shape[1] // HD
    group = H // KVH
    kv_width = max(KVD // feat_count, HD)
    kv_start = feat_index * head_count // group * HD
    k_slice = lax.dynamic_slice_in_dim(k_weight, kv_start, kv_width, 1)
    v_slice = lax.dynamic_slice_in_dim(v_weight, kv_start, kv_width, 1)
    q_panel, k_panel, v_panel, o_panel = (
        lax.all_gather(q_weight, "seq", axis=0, tiled=True),
        lax.all_gather(k_slice, "seq", axis=0, tiled=True),
        lax.all_gather(v_slice, "seq", axis=0, tiled=True),
        lax.all_gather(o_weight, "seq", axis=0, tiled=True),
    )
    query_count = tokens.shape[0]
    query_start = lax.axis_index("seq") * query_count
    positions = query_start + jnp.arange(query_count, dtype=jnp.int32)
    piece = lax.all_gather(tokens, "feat", axis=1, tiled=True)
    q_raw, k_raw, v_raw = tuple(
        (
            jnp.dot(piece, panel, preferred_element_type=jnp.float32)
            for panel in (q_panel, k_panel, v_panel)
        )
    )
    queries = rotary(q_raw, positions).astype(jnp.bfloat16)
    keys = rotary(k_raw, positions).astype(jnp.bfloat16)
    values = v_raw.astype(jnp.bfloat16)
    kv_heads = kv_width // HD
    context = (queries, segment_ids, query_start, kv_heads)
    groups = head_count // kv_heads
    initial = (
        jnp.full((kv_heads, groups, query_count), -1e30, jnp.float32),
        jnp.zeros((kv_heads, groups, query_count), jnp.float32),
        jnp.zeros((kv_heads, groups, query_count, HD), jnp.float32),
    )
    final = fold_piece(
        initial,
        (
            lax.all_gather(keys, "seq", axis=0, tiled=True),
            lax.all_gather(values, "seq", axis=0, tiled=True),
            lax.all_gather(segment_ids, "seq", axis=0, tiled=True),
        ),
        context,
    )
    running_sum = final[1]
    weighted = final[2]
    attended = (
        (weighted / running_sum[..., None])
        .transpose(2, 0, 1, 3)
        .reshape(query_count, -1)
        .astype(jnp.bfloat16)
    )
    result = jnp.dot(
        lax.all_gather(attended, "feat", axis=1, tiled=True),
        o_panel,
        preferred_element_type=jnp.float32,
    )
    return result.astype(jnp.bfloat16)


def solution(mesh):
    in_specs = (
        P("seq", "feat"),
        P("seq"),
        P("seq", "feat"),
        P("seq", None),
        P("seq", None),
        P("seq", "feat"),
    )
    out_specs = P("seq", "feat")
    return jax.shard_map(local, mesh=mesh, in_specs=in_specs, out_specs=out_specs, check_vma=False)
```

profile of v0, /device:TPU:25, one launch (start us, length us, event | category | flops | bytes accessed | tf_op | source)
XLA Modules:
  0.0 970.9 jit_solution(14138776308825019925)
XLA Ops:
  11.7 46.5 %all-gather.9.cloned.1.call-done = bf16[4096,256]{1,0:T(8,128)(2,1)} async-done(((bf16[512,256]{1,0:T(8,128)(2,1)}), bf16[4096,256]{1,0:T(8,128)(2,1)}) %all-gather.9.cloned.1.call-update) | async-done | bytes 2097168 | tf_op jit(solution)/shard_map/all_gather | solution.py:96
  58.2 60.4 %all-gather.11.cloned.1.call-done = bf16[1024,4096]{1,0:T(8,128)(2,1)} async-done(((bf16[1024,1024]{1,0:T(8,128)(2,1)}), bf16[1024,4096]{1,0:T(8,128)(2,1)}) %all-gather.11.cloned.1.call-update) | async-done | bytes 8388624 | tf_op jit(solution)/shard_map/all_gather | solution.py:103
  118.6 6.4 convolution_bitcast_fusion
  131.3 36.9 %all-gather.17.cloned.1.call-done = bf16[4096,256]{1,0:T(8,128)(2,1)} async-done(((bf16[512,256]{1,0:T(8,128)(2,1)}), bf16[4096,256]{1,0:T(8,128)(2,1)}) %all-gather.17.cloned.1.call-update) | async-done | bytes 2097168 | tf_op jit(solution)/shard_map/all_gather | solution.py:97
  168.2 7.2 fusion.21
  176.2 22.9 %all_gather.27 = s32[8192]{0:T(1024)S(1)} all-gather(s32[1024]{0:T(1024)S(1)} %copy-done.5), channel_id=1, replica_groups=mesh['seq'=8,'feat'=4] {'seq'}, dimensions={0}, use_global_device_ids=true | all-gather | bytes 36864 | tf_op jit(solution)/shard_map/all_gather | solution.py:126
  199.2 94.6 %all-gather.15.cloned.1.call-done = bf16[4096,1024]{1,0:T(8,128)(2,1)} async-done(((bf16[512,1024]{1,0:T(8,128)(2,1)}), bf16[4096,1024]{1,0:T(8,128)(2,1)}) %all-gather.15.cloned.1.call-update) | async-done | bytes 8388624 | tf_op jit(solution)/shard_map/all_gather | solution.py:95
  293.8 15.1 %fusion.45 = f32[1024,1024]{0,1:T(8,128)} fusion(bf16[1024,4096]{1,0:T(8,128)(2,1)} %all-gather.11.cloned.1.call-done, bf16[4096,1024]{1,0:T(8,128)(2,1)} %all-gather.15.cloned.1.call-done), kind=kOutput, calls=%fused_computation.68 | convolution fusion | flops 8589934592 | bytes 20971520 | tf_op jit(solution)/shard_map/dot_general | solution.py:106
  308.9 5.9 reshape.255
  314.8 9.1 fusion.43
  323.9 4.6 copy.54
  328.5 6.1 copy.53
  334.6 9.5 fusion.18
  355.3 12.3 %all-gather.13.cloned.1.call-done = bf16[8192,256]{0,1:T(8,128)(2,1)} async-done(((bf16[1024,256]{0,1:T(8,128)(2,1)}), bf16[8192,256]{0,1:T(8,128)(2,1)}) %all-gather.13.cloned.1.call-update) | async-done | bytes 4194320 | tf_op jit(solution)/shard_map/all_gather | solution.py:124
  367.6 73.7 %all-gather.19.cloned.1.call-done = bf16[8192,256]{0,1:T(8,128)(2,1)} async-done(((bf16[1024,256]{0,1:T(8,128)(2,1)}), bf16[8192,256]{0,1:T(8,128)(2,1)}) %all-gather.19.cloned.1.call-update) | async-done | bytes 4194320 | tf_op jit(solution)/shard_map/all_gather | solution.py:125
  443.7 382.9 %while.17 = (s32[]{:T(128)}, f32[2,4,1024]{2,1,0:T(4,128)S(1)}, f32[2,4,1024]{2,1,0:T(4,128)S(1)}, f32[2,4,1024,128]{3,2,1,0:T(8,128)}, s32[]{:T(128)}, /*index=...) while((s32[]{:T(128)}, f32[2,4,1024]{2,1,0:T(4,128)S(1)}, ...), condition=%wide.region_5.6_spmd, body=%wide.region_0.5_spmd.sunk | while | flops 4409280512 | bytes 158892464 | solution.py:82
  443.7 55.0 %conditional.2 = ((f32[2,4,1024]{2,1,0:T(4,128)S(1)}, f32[2,4,1024]{2,1,0:T(4,128)S(1)}, f32[2,4,1024,128]{3,2,1,0:T(8,128)})) conditional(s32[]{:T(128)} %convert_element_type.101, (f32[2,4,1024]{2,1,0:T(4,128)S(1)}, f32[2,4,1024]{2,1,0:T(4,128)S(1)}, f32[2,4,1024,128]{3,2,1,0:T(8,128)}) %tuple.60, (s32[]{:T(128)}, s32[]{:T(128)}, ...), branch_computations={%region_1.1_spmd, %region_2.4_spmd} | conditional | flops 4409280512 | bytes 158892192 | solution.py:73
  449.8 15.6 %fusion = (f32[2,4,1024]{2,1,0:T(4,128)S(1)}, f32[2,1024,1024,4]{2,1,3,0:T(8,128)}) fusion(pred[1024,1024]{0,1:T(8,128)(4,1)S(1)} %compare_and_fusion, bf16[1024,2,128,1]{0,2,3,1:T(8,128)(2,1)} %bitcast.55, bf16[1024,2,4,128]{3,2,1,0:T(4,128)(2,1)} %reshape.250), kind=kOutput, calls=%fused_computation.2 | convolution fusion | flops 2172641280 | bytes 37257216 | tf_op jit(solution)/shard_map/while/body/eval_jaxpr/cond/branch_1_fun/rngd,knd->ngrk/dot_general | solution.py:39
  465.5 15.4 %fusion.2 = f32[2,4,1024]{2,1,0:T(4,128)S(1)} fusion(f32[2,1024,1024,4]{2,1,3,0:T(8,128)} %get-tuple-element.406, f32[2,4,1024]{2,1,0:T(4,128)S(1)} %max.5, pred[1024,1024]{0,1:T(8,128)(4,1)S(1)} %compare_and_fusion), kind=kLoop, calls=%fused_computation.4 | loop fusion | flops 41934848 | bytes 34668544 | tf_op jit(solution)/shard_map/while/body/eval_jaxpr/cond/branch_1_fun/reduce_sum | solution.py:51
  481.0 15.7 %multiply_add_fusion = f32[2,4,1024,128]{3,2,1,0:T(8,128)S(1)} fusion(f32[2,4,1024,128]{3,2,1,0:T(8,128)S(1)} %copy-done.2, bf16[1024,2,128,1]{0,2,3,1:T(8,128)(2,1)S(1)} %bitcast.54, f32[2,1024,1024,4]{2,1,3,0:T(8,128)} %get-tuple-element.406, f32[2,4,1024]{2,1,0:T(4,128)S(1)} %max.5, pred[1024,1024]{0,1:T(8,128)(4,1)S(1)} %compare_and_fusion, ...), kind=kOutput, calls=%fused_computation.7 | convolution fusion | flops 2191523840 | bytes 43581440 | tf_op jit(solution)/shard_map/while/body/eval_jaxpr/cond/branch_1_fun/ngrk,knd->ngrd/dot_general | solution.py:52
  498.7 55.0 %conditional.2 = ((f32[2,4,1024]{2,1,0:T(4,128)S(1)}, f32[2,4,1024]{2,1,0:T(4,128)S(1)}, f32[2,4,1024,128]{3,2,1,0:T(8,128)})) conditional(s32[]{:T(128)} %convert_element_type.101, (f32[2,4,1024]{2,1,0:T(4,128)S(1)}, f32[2,4,1024]{2,1,0:T(4,128)S(1)}, f32[2,4,1024,128]{3,2,1,0:T(8,128)}) %tuple.60, (s32[]{:T(128)}, s32[]{:T(128)}, ...), branch_computations={%region_1.1_spmd, %region_2.4_spmd} | conditional | flops 4409280512 | bytes 158892192 | solution.py:73
  504.8 15.4 %fusion = (f32[2,4,1024]{2,1,0:T(4,128)S(1)}, f32[2,1024,1024,4]{2,1,3,0:T(8,128)}) fusion(pred[1024,1024]{0,1:T(8,128)(4,1)S(1)} %compare_and_fusion, bf16[1024,2,128,1]{0,2,3,1:T(8,128)(2,1)} %bitcast.55, bf16[1024,2,4,128]{3,2,1,0:T(4,128)(2,1)} %reshape.250), kind=kOutput, calls=%fused_computation.2 | convolution fusion | flops 2172641280 | bytes 37257216 | tf_op jit(solution)/shard_map/while/body/eval_jaxpr/cond/branch_1_fun/rngd,knd->ngrk/dot_general | solution.py:39
  520.3 15.3 %fusion.2 = f32[2,4,1024]{2,1,0:T(4,128)S(1)} fusion(f32[2,1024,1024,4]{2,1,3,0:T(8,128)} %get-tuple-element.406, f32[2,4,1024]{2,1,0:T(4,128)S(1)} %max.5, pred[1024,1024]{0,1:T(8,128)(4,1)S(1)} %compare_and_fusion), kind=kLoop, calls=%fused_computation.4 | loop fusion | flops 41934848 | bytes 34668544 | tf_op jit(solution)/shard_map/while/body/eval_jaxpr/cond/branch_1_fun/reduce_sum | solution.py:51
  535.7 15.9 %multiply_add_fusion = f32[2,4,1024,128]{3,2,1,0:T(8,128)S(1)} fusion(f32[2,4,1024,128]{3,2,1,0:T(8,128)S(1)} %copy-done.2, bf16[1024,2,128,1]{0,2,3,1:T(8,128)(2,1)S(1)} %bitcast.54, f32[2,1024,1024,4]{2,1,3,0:T(8,128)} %get-tuple-element.406, f32[2,4,1024]{2,1,0:T(4,128)S(1)} %max.5, pred[1024,1024]{0,1:T(8,128)(4,1)S(1)} %compare_and_fusion, ...), kind=kOutput, calls=%fused_computation.7 | convolution fusion | flops 2191523840 | bytes 43581440 | tf_op jit(solution)/shard_map/while/body/eval_jaxpr/cond/branch_1_fun/ngrk,knd->ngrd/dot_general | solution.py:52
  553.6 54.6 %conditional.2 = ((f32[2,4,1024]{2,1,0:T(4,128)S(1)}, f32[2,4,1024]{2,1,0:T(4,128)S(1)}, f32[2,4,1024,128]{3,2,1,0:T(8,128)})) conditional(s32[]{:T(128)} %convert_element_type.101, (f32[2,4,1024]{2,1,0:T(4,128)S(1)}, f32[2,4,1024]{2,1,0:T(4,128)S(1)}, f32[2,4,1024,128]{3,2,1,0:T(8,128)}) %tuple.60, (s32[]{:T(128)}, s32[]{:T(128)}, ...), branch_computations={%region_1.1_spmd, %region_2.4_spmd} | conditional | flops 4409280512 | bytes 158892192 | solution.py:73
  559.8 15.4 %fusion = (f32[2,4,1024]{2,1,0:T(4,128)S(1)}, f32[2,1024,1024,4]{2,1,3,0:T(8,128)}) fusion(pred[1024,1024]{0,1:T(8,128)(4,1)S(1)} %compare_and_fusion, bf16[1024,2,128,1]{0,2,3,1:T(8,128)(2,1)} %bitcast.55, bf16[1024,2,4,128]{3,2,1,0:T(4,128)(2,1)} %reshape.250), kind=kOutput, calls=%fused_computation.2 | convolution fusion | flops 2172641280 | bytes 37257216 | tf_op jit(solution)/shard_map/while/body/eval_jaxpr/cond/branch_1_fun/rngd,knd->ngrk/dot_general | solution.py:39
  575.2 15.3 %fusion.2 = f32[2,4,1024]{2,1,0:T(4,128)S(1)} fusion(f32[2,1024,1024,4]{2,1,3,0:T(8,128)} %get-tuple-element.406, f32[2,4,1024]{2,1,0:T(4,128)S(1)} %max.5, pred[1024,1024]{0,1:T(8,128)(4,1)S(1)} %compare_and_fusion), kind=kLoop, calls=%fused_computation.4 | loop fusion | flops 41934848 | bytes 34668544 | tf_op jit(solution)/shard_map/while/body/eval_jaxpr/cond/branch_1_fun/reduce_sum | solution.py:51
  590.5 15.7 %multiply_add_fusion = f32[2,4,1024,128]{3,2,1,0:T(8,128)S(1)} fusion(f32[2,4,1024,128]{3,2,1,0:T(8,128)S(1)} %copy-done.2, bf16[1024,2,128,1]{0,2,3,1:T(8,128)(2,1)S(1)} %bitcast.54, f32[2,1024,1024,4]{2,1,3,0:T(8,128)} %get-tuple-element.406, f32[2,4,1024]{2,1,0:T(4,128)S(1)} %max.5, pred[1024,1024]{0,1:T(8,128)(4,1)S(1)} %compare_and_fusion, ...), kind=kOutput, calls=%fused_computation.7 | convolution fusion | flops 2191523840 | bytes 43581440 | tf_op jit(solution)/shard_map/while/body/eval_jaxpr/cond/branch_1_fun/ngrk,knd->ngrd/dot_general | solution.py:52
  608.2 54.6 %conditional.2 = ((f32[2,4,1024]{2,1,0:T(4,128)S(1)}, f32[2,4,1024]{2,1,0:T(4,128)S(1)}, f32[2,4,1024,128]{3,2,1,0:T(8,128)})) conditional(s32[]{:T(128)} %convert_element_type.101, (f32[2,4,1024]{2,1,0:T(4,128)S(1)}, f32[2,4,1024]{2,1,0:T(4,128)S(1)}, f32[2,4,1024,128]{3,2,1,0:T(8,128)}) %tuple.60, (s32[]{:T(128)}, s32[]{:T(128)}, ...), branch_computations={%region_1.1_spmd, %region_2.4_spmd} | conditional | flops 4409280512 | bytes 158892192 | solution.py:73
  614.3 15.4 %fusion = (f32[2,4,1024]{2,1,0:T(4,128)S(1)}, f32[2,1024,1024,4]{2,1,3,0:T(8,128)}) fusion(pred[1024,1024]{0,1:T(8,128)(4,1)S(1)} %compare_and_fusion, bf16[1024,2,128,1]{0,2,3,1:T(8,128)(2,1)} %bitcast.55, bf16[1024,2,4,128]{3,2,1,0:T(4,128)(2,1)} %reshape.250), kind=kOutput, calls=%fused_computation.2 | convolution fusion | flops 2172641280 | bytes 37257216 | tf_op jit(solution)/shard_map/while/body/eval_jaxpr/cond/branch_1_fun/rngd,knd->ngrk/dot_general | solution.py:39
  629.8 15.3 %fusion.2 = f32[2,4,1024]{2,1,0:T(4,128)S(1)} fusion(f32[2,1024,1024,4]{2,1,3,0:T(8,128)} %get-tuple-element.406, f32[2,4,1024]{2,1,0:T(4,128)S(1)} %max.5, pred[1024,1024]{0,1:T(8,128)(4,1)S(1)} %compare_and_fusion), kind=kLoop, calls=%fused_computation.4 | loop fusion | flops 41934848 | bytes 34668544 | tf_op jit(solution)/shard_map/while/body/eval_jaxpr/cond/branch_1_fun/reduce_sum | solution.py:51
  645.1 15.7 %multiply_add_fusion = f32[2,4,1024,128]{3,2,1,0:T(8,128)S(1)} fusion(f32[2,4,1024,128]{3,2,1,0:T(8,128)S(1)} %copy-done.2, bf16[1024,2,128,1]{0,2,3,1:T(8,128)(2,1)S(1)} %bitcast.54, f32[2,1024,1024,4]{2,1,3,0:T(8,128)} %get-tuple-element.406, f32[2,4,1024]{2,1,0:T(4,128)S(1)} %max.5, pred[1024,1024]{0,1:T(8,128)(4,1)S(1)} %compare_and_fusion, ...), kind=kOutput, calls=%fused_computation.7 | convolution fusion | flops 2191523840 | bytes 43581440 | tf_op jit(solution)/shard_map/while/body/eval_jaxpr/cond/branch_1_fun/ngrk,knd->ngrd/dot_general | solution.py:52
  662.8 54.6 %conditional.2 = ((f32[2,4,1024]{2,1,0:T(4,128)S(1)}, f32[2,4,1024]{2,1,0:T(4,128)S(1)}, f32[2,4,1024,128]{3,2,1,0:T(8,128)})) conditional(s32[]{:T(128)} %convert_element_type.101, (f32[2,4,1024]{2,1,0:T(4,128)S(1)}, f32[2,4,1024]{2,1,0:T(4,128)S(1)}, f32[2,4,1024,128]{3,2,1,0:T(8,128)}) %tuple.60, (s32[]{:T(128)}, s32[]{:T(128)}, ...), branch_computations={%region_1.1_spmd, %region_2.4_spmd} | conditional | flops 4409280512 | bytes 158892192 | solution.py:73
  668.9 15.4 %fusion = (f32[2,4,1024]{2,1,0:T(4,128)S(1)}, f32[2,1024,1024,4]{2,1,3,0:T(8,128)}) fusion(pred[1024,1024]{0,1:T(8,128)(4,1)S(1)} %compare_and_fusion, bf16[1024,2,128,1]{0,2,3,1:T(8,128)(2,1)} %bitcast.55, bf16[1024,2,4,128]{3,2,1,0:T(4,128)(2,1)} %reshape.250), kind=kOutput, calls=%fused_computation.2 | convolution fusion | flops 2172641280 | bytes 37257216 | tf_op jit(solution)/shard_map/while/body/eval_jaxpr/cond/branch_1_fun/rngd,knd->ngrk/dot_general | solution.py:39
  684.4 15.3 %fusion.2 = f32[2,4,1024]{2,1,0:T(4,128)S(1)} fusion(f32[2,1024,1024,4]{2,1,3,0:T(8,128)} %get-tuple-element.406, f32[2,4,1024]{2,1,0:T(4,128)S(1)} %max.5, pred[1024,1024]{0,1:T(8,128)(4,1)S(1)} %compare_and_fusion), kind=kLoop, calls=%fused_computation.4 | loop fusion | flops 41934848 | bytes 34668544 | tf_op jit(solution)/shard_map/while/body/eval_jaxpr/cond/branch_1_fun/reduce_sum | solution.py:51
  699.7 15.7 %multiply_add_fusion = f32[2,4,1024,128]{3,2,1,0:T(8,128)S(1)} fusion(f32[2,4,1024,128]{3,2,1,0:T(8,128)S(1)} %copy-done.2, bf16[1024,2,128,1]{0,2,3,1:T(8,128)(2,1)S(1)} %bitcast.54, f32[2,1024,1024,4]{2,1,3,0:T(8,128)} %get-tuple-element.406, f32[2,4,1024]{2,1,0:T(4,128)S(1)} %max.5, pred[1024,1024]{0,1:T(8,128)(4,1)S(1)} %compare_and_fusion, ...), kind=kOutput, calls=%fused_computation.7 | convolution fusion | flops 2191523840 | bytes 43581440 | tf_op jit(solution)/shard_map/while/body/eval_jaxpr/cond/branch_1_fun/ngrk,knd->ngrd/dot_general | solution.py:52
  717.4 54.6 %conditional.2 = ((f32[2,4,1024]{2,1,0:T(4,128)S(1)}, f32[2,4,1024]{2,1,0:T(4,128)S(1)}, f32[2,4,1024,128]{3,2,1,0:T(8,128)})) conditional(s32[]{:T(128)} %convert_element_type.101, (f32[2,4,1024]{2,1,0:T(4,128)S(1)}, f32[2,4,1024]{2,1,0:T(4,128)S(1)}, f32[2,4,1024,128]{3,2,1,0:T(8,128)}) %tuple.60, (s32[]{:T(128)}, s32[]{:T(128)}, ...), branch_computations={%region_1.1_spmd, %region_2.4_spmd} | conditional | flops 4409280512 | bytes 158892192 | solution.py:73
  723.5 15.4 %fusion = (f32[2,4,1024]{2,1,0:T(4,128)S(1)}, f32[2,1024,1024,4]{2,1,3,0:T(8,128)}) fusion(pred[1024,1024]{0,1:T(8,128)(4,1)S(1)} %compare_and_fusion, bf16[1024,2,128,1]{0,2,3,1:T(8,128)(2,1)} %bitcast.55, bf16[1024,2,4,128]{3,2,1,0:T(4,128)(2,1)} %reshape.250), kind=kOutput, calls=%fused_computation.2 | convolution fusion | flops 2172641280 | bytes 37257216 | tf_op jit(solution)/shard_map/while/body/eval_jaxpr/cond/branch_1_fun/rngd,knd->ngrk/dot_general | solution.py:39
  739.0 15.3 %fusion.2 = f32[2,4,1024]{2,1,0:T(4,128)S(1)} fusion(f32[2,1024,1024,4]{2,1,3,0:T(8,128)} %get-tuple-element.406, f32[2,4,1024]{2,1,0:T(4,128)S(1)} %max.5, pred[1024,1024]{0,1:T(8,128)(4,1)S(1)} %compare_and_fusion), kind=kLoop, calls=%fused_computation.4 | loop fusion | flops 41934848 | bytes 34668544 | tf_op jit(solution)/shard_map/while/body/eval_jaxpr/cond/branch_1_fun/reduce_sum | solution.py:51
  754.3 15.7 %multiply_add_fusion = f32[2,4,1024,128]{3,2,1,0:T(8,128)S(1)} fusion(f32[2,4,1024,128]{3,2,1,0:T(8,128)S(1)} %copy-done.2, bf16[1024,2,128,1]{0,2,3,1:T(8,128)(2,1)S(1)} %bitcast.54, f32[2,1024,1024,4]{2,1,3,0:T(8,128)} %get-tuple-element.406, f32[2,4,1024]{2,1,0:T(4,128)S(1)} %max.5, pred[1024,1024]{0,1:T(8,128)(4,1)S(1)} %compare_and_fusion, ...), kind=kOutput, calls=%fused_computation.7 | convolution fusion | flops 2191523840 | bytes 43581440 | tf_op jit(solution)/shard_map/while/body/eval_jaxpr/cond/branch_1_fun/ngrk,knd->ngrd/dot_general | solution.py:52
  772.0 54.6 %conditional.2 = ((f32[2,4,1024]{2,1,0:T(4,128)S(1)}, f32[2,4,1024]{2,1,0:T(4,128)S(1)}, f32[2,4,1024,128]{3,2,1,0:T(8,128)})) conditional(s32[]{:T(128)} %convert_element_type.101, (f32[2,4,1024]{2,1,0:T(4,128)S(1)}, f32[2,4,1024]{2,1,0:T(4,128)S(1)}, f32[2,4,1024,128]{3,2,1,0:T(8,128)}) %tuple.60, (s32[]{:T(128)}, s32[]{:T(128)}, ...), branch_computations={%region_1.1_spmd, %region_2.4_spmd} | conditional | flops 4409280512 | bytes 158892192 | solution.py:73
  778.1 15.4 %fusion = (f32[2,4,1024]{2,1,0:T(4,128)S(1)}, f32[2,1024,1024,4]{2,1,3,0:T(8,128)}) fusion(pred[1024,1024]{0,1:T(8,128)(4,1)S(1)} %compare_and_fusion, bf16[1024,2,128,1]{0,2,3,1:T(8,128)(2,1)} %bitcast.55, bf16[1024,2,4,128]{3,2,1,0:T(4,128)(2,1)} %reshape.250), kind=kOutput, calls=%fused_computation.2 | convolution fusion | flops 2172641280 | bytes 37257216 | tf_op jit(solution)/shard_map/while/body/eval_jaxpr/cond/branch_1_fun/rngd,knd->ngrk/dot_general | solution.py:39
  793.6 15.3 %fusion.2 = f32[2,4,1024]{2,1,0:T(4,128)S(1)} fusion(f32[2,1024,1024,4]{2,1,3,0:T(8,128)} %get-tuple-element.406, f32[2,4,1024]{2,1,0:T(4,128)S(1)} %max.5, pred[1024,1024]{0,1:T(8,128)(4,1)S(1)} %compare_and_fusion), kind=kLoop, calls=%fused_computation.4 | loop fusion | flops 41934848 | bytes 34668544 | tf_op jit(solution)/shard_map/while/body/eval_jaxpr/cond/branch_1_fun/reduce_sum | solution.py:51
  808.9 15.7 %multiply_add_fusion = f32[2,4,1024,128]{3,2,1,0:T(8,128)S(1)} fusion(f32[2,4,1024,128]{3,2,1,0:T(8,128)S(1)} %copy-done.2, bf16[1024,2,128,1]{0,2,3,1:T(8,128)(2,1)S(1)} %bitcast.54, f32[2,1024,1024,4]{2,1,3,0:T(8,128)} %get-tuple-element.406, f32[2,4,1024]{2,1,0:T(4,128)S(1)} %max.5, pred[1024,1024]{0,1:T(8,128)(4,1)S(1)} %compare_and_fusion, ...), kind=kOutput, calls=%fused_computation.7 | convolution fusion | flops 2191523840 | bytes 43581440 | tf_op jit(solution)/shard_map/while/body/eval_jaxpr/cond/branch_1_fun/ngrk,knd->ngrd/dot_general | solution.py:52
  826.6 5.4 copy.43
  832.0 4.1 divide_convert_fusion
  836.2 113.1 %all-gather.21.cloned.1.call-done = bf16[1024,4096]{0,1:T(8,128)(2,1)} async-done(((bf16[1024,1024]{0,1:T(8,128)(2,1)}), bf16[1024,4096]{0,1:T(8,128)(2,1)}) %all-gather.21.cloned.1.call-update) | async-done | bytes 8388624 | tf_op jit(solution)/shard_map/all_gather | solution.py:139
  949.3 14.8 %convolution_convert_fusion = bf16[1024,1024]{1,0:T(8,128)(2,1)} fusion(bf16[1024,4096]{0,1:T(8,128)(2,1)} %all-gather.21.cloned.1.call-done, bf16[4096,1024]{1,0:T(8,128)(2,1)} %all-gather.23.cloned.1.call-done), kind=kOutput, calls=%fused_computation.32 | convolution fusion | flops 8590983168 | bytes 18874368 | tf_op jit(solution)/shard_map/dot_general | solution.py:138
  (142 shorter events, 83.0 us)
Async XLA Ops:
  6.5 1.2 copy-start
  6.5 51.7 %all-gather.9.cloned.1.call-start = ((), (), s32[]{:S(2)}) async-start(), calls=%async_computation | async-start | bytes 2359296 | tf_op jit(solution)/shard_map/all_gather | solution.py:96
  8.5 110.1 %all-gather.11.cloned.1.call-start = ((), (), s32[]{:S(2)}) async-start(), calls=%async_computation.1 | async-start | bytes 10485760 | tf_op jit(solution)/shard_map/all_gather | solution.py:103
  9.3 158.9 %all-gather.17.cloned.1.call-start = ((), (), s32[]{:S(2)}) async-start(), calls=%async_computation.4 | async-start | bytes 2359296 | tf_op jit(solution)/shard_map/all_gather | solution.py:97
  11.0 282.8 %all-gather.15.cloned.1.call-start = ((), (), s32[]{:S(2)}) async-start(), calls=%async_computation.3 | async-start | bytes 9437184 | tf_op jit(solution)/shard_map/all_gather | solution.py:95
  11.6 356.0 %all-gather.13.cloned.1.call-start = ((), (), s32[]{:S(2)}) async-start(), calls=%async_computation.2 | async-start | bytes 4718592 | tf_op jit(solution)/shard_map/all_gather | solution.py:124
  131.2 45.0 %copy-start.5 = (s32[1024]{0:T(1024)S(1)}, s32[1024]{0:T(1024)}, u32[]{:S(2)}) copy-start(s32[1024]{0:T(1024)} %param.11) | copy-start | bytes 12292
  131.2 310.1 %all-gather.19.cloned.1.call-start = ((), (), s32[]{:S(2)}) async-start(), calls=%async_computation.5 | async-start | bytes 4718592 | tf_op jit(solution)/shard_map/all_gather | solution.py:125
  175.4 660.7 %all-gather.23.cloned.1.call-start = ((), (), s32[]{:S(2)}) async-start(), calls=%async_computation.7 | async-start | bytes 9437184 | tf_op jit(solution)/shard_map/all_gather | solution.py:98
  176.2 773.1 %all-gather.21.cloned.1.call-start = ((), (), s32[]{:S(2)}) async-start(), calls=%async_computation.6 | async-start | bytes 10485760 | tf_op jit(solution)/shard_map/all_gather | solution.py:139
  465.5 15.5 %copy-start.2 = (f32[2,4,1024,128]{3,2,1,0:T(8,128)S(1)}, f32[2,4,1024,128]{3,2,1,0:T(8,128)}, u32[]{:S(2)}) copy-start(f32[2,4,1024,128]{3,2,1,0:T(8,128)} %get-tuple-element.305) | copy-start | bytes 12582916 | tf_op jit(solution)/shard_map/while/body/eval_jaxpr/cond
  465.5 15.5 %copy-start.4 = (bf16[1024,256]{0,1:T(8,128)(2,1)S(1)}, bf16[1024,256]{0,1:T(8,128)(2,1)}, u32[]{:S(2)}) copy-start(bf16[1024,256]{0,1:T(8,128)(2,1)} %get-tuple-element.409) | copy-start | bytes 1572868 | tf_op jit(solution)/shard_map/while/body/eval_jaxpr/cond
  496.6 2.0 copy-start.3
  520.2 15.4 %copy-start.2 = (f32[2,4,1024,128]{3,2,1,0:T(8,128)S(1)}, f32[2,4,1024,128]{3,2,1,0:T(8,128)}, u32[]{:S(2)}) copy-start(f32[2,4,1024,128]{3,2,1,0:T(8,128)} %get-tuple-element.305) | copy-start | bytes 12582916 | tf_op jit(solution)/shard_map/while/body/eval_jaxpr/cond
  520.3 15.4 %copy-start.4 = (bf16[1024,256]{0,1:T(8,128)(2,1)S(1)}, bf16[1024,256]{0,1:T(8,128)(2,1)}, u32[]{:S(2)}) copy-start(bf16[1024,256]{0,1:T(8,128)(2,1)} %get-tuple-element.409) | copy-start | bytes 1572868 | tf_op jit(solution)/shard_map/while/body/eval_jaxpr/cond
  551.6 2.0 copy-start.3
  575.2 15.4 %copy-start.2 = (f32[2,4,1024,128]{3,2,1,0:T(8,128)S(1)}, f32[2,4,1024,128]{3,2,1,0:T(8,128)}, u32[]{:S(2)}) copy-start(f32[2,4,1024,128]{3,2,1,0:T(8,128)} %get-tuple-element.305) | copy-start | bytes 12582916 | tf_op jit(solution)/shard_map/while/body/eval_jaxpr/cond
  575.2 15.3 %copy-start.4 = (bf16[1024,256]{0,1:T(8,128)(2,1)S(1)}, bf16[1024,256]{0,1:T(8,128)(2,1)}, u32[]{:S(2)}) copy-start(bf16[1024,256]{0,1:T(8,128)(2,1)} %get-tuple-element.409) | copy-start | bytes 1572868 | tf_op jit(solution)/shard_map/while/body/eval_jaxpr/cond
  606.2 2.0 copy-start.3
  629.7 15.4 %copy-start.2 = (f32[2,4,1024,128]{3,2,1,0:T(8,128)S(1)}, f32[2,4,1024,128]{3,2,1,0:T(8,128)}, u32[]{:S(2)}) copy-start(f32[2,4,1024,128]{3,2,1,0:T(8,128)} %get-tuple-element.305) | copy-start | bytes 12582916 | tf_op jit(solution)/shard_map/while/body/eval_jaxpr/cond
  629.8 15.3 %copy-start.4 = (bf16[1024,256]{0,1:T(8,128)(2,1)S(1)}, bf16[1024,256]{0,1:T(8,128)(2,1)}, u32[]{:S(2)}) copy-start(bf16[1024,256]{0,1:T(8,128)(2,1)} %get-tuple-element.409) | copy-start | bytes 1572868 | tf_op jit(solution)/shard_map/while/body/eval_jaxpr/cond
  660.8 2.0 copy-start.3
  684.3 15.4 %copy-start.2 = (f32[2,4,1024,128]{3,2,1,0:T(8,128)S(1)}, f32[2,4,1024,128]{3,2,1,0:T(8,128)}, u32[]{:S(2)}) copy-start(f32[2,4,1024,128]{3,2,1,0:T(8,128)} %get-tuple-element.305) | copy-start | bytes 12582916 | tf_op jit(solution)/shard_map/while/body/eval_jaxpr/cond
  684.4 15.3 %copy-start.4 = (bf16[1024,256]{0,1:T(8,128)(2,1)S(1)}, bf16[1024,256]{0,1:T(8,128)(2,1)}, u32[]{:S(2)}) copy-start(bf16[1024,256]{0,1:T(8,128)(2,1)} %get-tuple-element.409) | copy-start | bytes 1572868 | tf_op jit(solution)/shard_map/while/body/eval_jaxpr/cond
  715.4 2.0 copy-start.3
  738.9 15.4 %copy-start.2 = (f32[2,4,1024,128]{3,2,1,0:T(8,128)S(1)}, f32[2,4,1024,128]{3,2,1,0:T(8,128)}, u32[]{:S(2)}) copy-start(f32[2,4,1024,128]{3,2,1,0:T(8,128)} %get-tuple-element.305) | copy-start | bytes 12582916 | tf_op jit(solution)/shard_map/while/body/eval_jaxpr/cond
  738.9 15.3 %copy-start.4 = (bf16[1024,256]{0,1:T(8,128)(2,1)S(1)}, bf16[1024,256]{0,1:T(8,128)(2,1)}, u32[]{:S(2)}) copy-start(bf16[1024,256]{0,1:T(8,128)(2,1)} %get-tuple-element.409) | copy-start | bytes 1572868 | tf_op jit(solution)/shard_map/while/body/eval_jaxpr/cond
  770.0 2.0 copy-start.3
  793.5 15.4 %copy-start.2 = (f32[2,4,1024,128]{3,2,1,0:T(8,128)S(1)}, f32[2,4,1024,128]{3,2,1,0:T(8,128)}, u32[]{:S(2)}) copy-start(f32[2,4,1024,128]{3,2,1,0:T(8,128)} %get-tuple-element.305) | copy-start | bytes 12582916 | tf_op jit(solution)/shard_map/while/body/eval_jaxpr/cond
  793.5 15.3 %copy-start.4 = (bf16[1024,256]{0,1:T(8,128)(2,1)S(1)}, bf16[1024,256]{0,1:T(8,128)(2,1)}, u32[]{:S(2)}) copy-start(bf16[1024,256]{0,1:T(8,128)(2,1)} %get-tuple-element.409) | copy-start | bytes 1572868 | tf_op jit(solution)/shard_map/while/body/eval_jaxpr/cond
  824.6 2.0 copy-start.3
  949.3 14.8 %copy-start.1 = (bf16[512,1024]{1,0:T(8,128)(2,1)S(1)}, bf16[512,1024]{1,0:T(8,128)(2,1)}, u32[]{:S(2)}) copy-start(bf16[512,1024]{1,0:T(8,128)(2,1)} %param.13) | copy-start | bytes 3145732
Sparse Core Ops, SparseCore 0:
  9.5 48.6 all-gather.8
  59.8 58.7 all-gather.10
  120.7 47.4 all-gather.16
  170.2 123.6 all-gather.14
  295.9 71.6 all-gather.12
  369.6 71.6 all-gather.18
  443.4 122.9 all-gather.22
  836.3 113.0 all-gather.20
where the time goes:
time: 974 us; the launch traced here: 971 us
  waiting for transfers between devices  440 us (45%)
  matrix products  261 us (27%)
  other arithmetic  132 us (14%)
  local copies, waits for them, and re-layouts  101 us (10%)
  blocking collectives  22.9 us (2%)
  between operations  13.6 us (1%)
    all_gather x1, waiting for transfers between devices, local(): lax.all_gather(attended, 'feat', axis=1, tiled=True)  113 us
    dot_general x7, matrix products, attend_block(): jnp.einsum('ngrk,knd->ngrd', probs.astype(jnp.bfloat16), value_heads, pre...  110 us
    dot_general x7, matrix products, attend_block(): jnp.einsum('rngd,knd->ngrk', query_heads, key_heads, preferred_element_ty...  108 us
    reduce_sum x7, other arithmetic, attend_block(): new_sum = running_sum * rescale + jnp.sum(probs, axis=-1)  107 us
    all_gather x1, waiting for transfers between devices, local(): lax.all_gather(q_weight, 'seq', axis=0, tiled=True)  94.6 us
    all_gather x1, waiting for transfers between devices, local(): lax.all_gather(values, 'seq', axis=0, tiled=True)  73.7 us
    all_gather x1, waiting for transfers between devices, local(): piece = lax.all_gather(tokens, 'feat', axis=1, tiled=True)  60.4 us
    all_gather x1, waiting for transfers between devices, local(): lax.all_gather(k_slice, 'seq', axis=0, tiled=True)  46.5 us
  transfers between devices with their start and end apart: 8, of which 7 were waited for; matrix products, arithmetic and copies ran while one was open for 48% of the time, Pallas kernels for 0%

commit v1 on v0

v1 whole, which is shorter than its diff:
```python
import functools
import math

import jax
import jax.numpy as jnp
from jax import lax
from jax.experimental import pallas as pl
from jax.experimental.pallas import tpu as pltpu
from jax.sharding import PartitionSpec as P

H = 32
KVH = 8
HD = 128
KVD = 1024
rope_base = 500000.0
VMEM_BYTES = 48 * 1024 * 1024
ROWS = 256
KEYS = 512


def rope_tables(positions):
    lane = jnp.arange(HD, dtype=jnp.int32)
    pair_index = (lane // 2).astype(jnp.float32)
    frequency = jnp.exp(-(2.0 * pair_index / HD) * math.log(rope_base))
    angle = positions.astype(jnp.float32)[:, None] * frequency[None, :]
    sign = jnp.where(lane % 2 == 0, -1.0, 1.0)
    return jnp.cos(angle), jnp.sin(angle) * sign[None, :]


def project_kernel(rope_tiles, x_ref, w_ref, cos_ref, sin_ref, o_ref):
    column = pl.program_id(0)
    rows = x_ref.shape[0]

    @pl.loop(0, rows // ROWS)
    def _(step):
        at = pl.ds(pl.multiple_of(step * ROWS, ROWS), ROWS)
        raw = jnp.dot(x_ref[at, :], w_ref[...], preferred_element_type=jnp.float32)

        def turned():
            cosine = cos_ref[at, :]
            sine = sin_ref[at, :]
            even = lax.broadcasted_iota(jnp.int32, (ROWS, HD), 1) % 2 == 0
            for head in range(w_ref.shape[1] // HD):
                part = raw[:, head * HD : (head + 1) * HD]
                other = jnp.where(
                    even, pltpu.roll(part, HD - 1, 1), pltpu.roll(part, 1, 1)
                )
                o_ref[at, head * HD : (head + 1) * HD] = (
                    part * cosine + other * sine
                ).astype(o_ref.dtype)

        def plain():
            o_ref[at, :] = raw.astype(o_ref.dtype)

        if rope_tiles is None:
            turned()
        else:
            pl.when(column < rope_tiles)(turned)
            pl.when(column >= rope_tiles)(plain)


def project(x, w, tables, tile, rope_tiles):
    rows, depth = x.shape
    columns = w.shape[1]
    return pl.pallas_call(
        functools.partial(project_kernel, rope_tiles),
        grid=(columns // tile,),
        out_shape=jax.ShapeDtypeStruct((rows, columns), jnp.bfloat16),
        in_specs=[
            pl.BlockSpec((rows, depth), lambda j: (0, 0)),
            pl.BlockSpec((depth, tile), lambda j: (0, j)),
            pl.BlockSpec((rows, HD), lambda j: (0, 0)),
            pl.BlockSpec((rows, HD), lambda j: (0, 0)),
        ],
        out_specs=pl.BlockSpec((rows, tile), lambda j: (0, j)),
        compiler_params=pltpu.CompilerParams(vmem_limit_bytes=VMEM_BYTES),
        cost_estimate=pl.CostEstimate(
            flops=2 * rows * depth * columns,
            bytes_accessed=2 * (rows * depth + depth * columns + rows * columns),
            transcendentals=0,
        ),
    )(x, w, *tables)


def attend_kernel(bounds, q_ref, k_ref, v_ref, start_ref, o_ref, m_ref, acc_ref):
    tile = pl.program_id(1)
    heads = q_ref.shape[1] // HD
    begin = bounds[0] + tile * ROWS
    first_start = bounds[1 + 2 * tile]
    last_start = bounds[2 + 2 * tile]
    low = first_start // KEYS
    high = (begin + ROWS - 1) // KEYS + 1
    full_low = jnp.minimum((last_start + KEYS - 1) // KEYS, high)
    full_high = jnp.clip((begin + 1) // KEYS, full_low, high)
    m_ref[...] = jnp.full(m_ref.shape, -1e30, jnp.float32)
    acc_ref[...] = jnp.zeros(acc_ref.shape, jnp.float32)
    ones = jnp.ones((KEYS, HD), jnp.bfloat16)

    def block(number, masked):
        at = pl.ds(pl.multiple_of(number * KEYS, KEYS), KEYS)
        keys = k_ref[at, :]
        values = jnp.concatenate([v_ref[at, :], ones], axis=1)
        if masked:
            key_at = number * KEYS + lax.broadcasted_iota(jnp.int32, (ROWS, KEYS), 1)
            query_at = begin + lax.broadcasted_iota(jnp.int32, (ROWS, KEYS), 0)
            allowed = (key_at <= query_at) & (key_at >= start_ref[...])
        for head in range(heads):
            scores = lax.dot_general(
                q_ref[:, head * HD : (head + 1) * HD],
                keys,
                (((1,), (1,)), ((), ())),
                preferred_element_type=jnp.float32,
            )
            if masked:
                scores = jnp.where(allowed, scores, -1e30)
            before = m_ref[head]
            after = jnp.maximum(before, jnp.max(scores, axis=1, keepdims=True))
            m_ref[head] = after
            probs = jnp.exp2(scores - jnp.concatenate([after] * (KEYS // HD), axis=1))
            rescale = jnp.exp2(before - after)
            acc_ref[head] = acc_ref[head] * jnp.concatenate(
                [rescale, rescale], axis=1
            ) + jnp.dot(
                probs.astype(jnp.bfloat16), values, preferred_element_type=jnp.float32
            )

    pl.loop(low, full_low)(lambda number: block(number, True))
    pl.loop(full_low, full_high)(lambda number: block(number, False))
    pl.loop(full_high, high)(lambda number: block(number, True))
    for head in range(heads):
        o_ref[:, head * HD : (head + 1) * HD] = (
            acc_ref[head, :, :HD] / acc_ref[head, :, HD:]
        ).astype(o_ref.dtype)


def attend(queries, kv, starts, query_start, kv_heads):
    rows, columns = queries.shape
    total = kv.shape[0]
    group = columns // HD // kv_heads
    tiles = rows // ROWS
    ends = jnp.stack([starts[::ROWS], starts[ROWS - 1 :: ROWS]], axis=1).reshape(-1)
    bounds = jnp.concatenate([query_start[None], ends]).astype(jnp.int32)
    return pl.pallas_call(
        attend_kernel,
        grid_spec=pltpu.PrefetchScalarGridSpec(
            num_scalar_prefetch=1,
            grid=(kv_heads, tiles),
            in_specs=[
                pl.BlockSpec((ROWS, group * HD), lambda h, t, b: (t, h)),
                pl.BlockSpec((total, HD), lambda h, t, b: (0, h)),
                pl.BlockSpec((total, HD), lambda h, t, b: (0, kv_heads + h)),
                pl.BlockSpec((ROWS, 1), lambda h, t, b: (t, 0)),
            ],
            out_specs=pl.BlockSpec((ROWS, group * HD), lambda h, t, b: (t, h)),
            scratch_shapes=[
                pltpu.VMEM((group, ROWS, HD), jnp.float32),
                pltpu.VMEM((group, ROWS, 2 * HD), jnp.float32),
            ],
        ),
        out_shape=jax.ShapeDtypeStruct((rows, columns), jnp.bfloat16),
        compiler_params=pltpu.CompilerParams(vmem_limit_bytes=VMEM_BYTES),
        cost_estimate=pl.CostEstimate(
            flops=2 * rows * columns * total,
            bytes_accessed=2 * (2 * rows * columns + 2 * total * kv_heads * HD),
            transcendentals=rows * columns // HD * total // 2,
        ),
    )(bounds, queries, kv, kv, starts[:, None])


def local(tokens, segment_ids, q_weight, k_weight, v_weight, o_weight):
    feat_count = lax.axis_size("feat")
    feat_index = lax.axis_index("feat")
    head_count = q_weight.shape[1] // HD
    group = H // KVH
    kv_width = max(KVD // feat_count, HD)
    kv_heads = kv_width // HD
    kv_start = feat_index * head_count // group * HD
    query_count = tokens.shape[0]
    query_start = lax.axis_index("seq") * query_count
    positions = query_start + jnp.arange(query_count, dtype=jnp.int32)
    cosine, sine = rope_tables(positions)
    factor = math.log2(math.e) / math.sqrt(HD)

    segments = lax.all_gather(segment_ids, "seq", axis=0, tiled=True)
    starts = jnp.sum(
        segments[None, :] < segment_ids[:, None], axis=1, dtype=jnp.int32
    )
    kv_slice = jnp.concatenate(
        [
            lax.dynamic_slice_in_dim(k_weight, kv_start, kv_width, 1),
            lax.dynamic_slice_in_dim(v_weight, kv_start, kv_width, 1),
        ],
        axis=1,
    )
    piece = lax.all_gather(tokens, "feat", axis=1, tiled=True)
    kv_panel = lax.all_gather(kv_slice, "seq", axis=0, tiled=True)
    kv_local = project(piece, kv_panel, (cosine, sine), kv_width, 1)
    q_panel = lax.all_gather(q_weight, "seq", axis=0, tiled=True)
    kv = lax.all_gather(kv_local, "seq", axis=0, tiled=True)
    queries = project(piece, q_panel, (cosine * factor, sine * factor), 256, None)
    o_panel = lax.all_gather(o_weight, "seq", axis=0, tiled=True)
    attended = attend(queries, kv, starts, query_start, kv_heads)
    result = jnp.dot(
        lax.all_gather(attended, "feat", axis=1, tiled=True),
        o_panel,
        preferred_element_type=jnp.float32,
    )
    return result.astype(jnp.bfloat16)


def solution(mesh):
    in_specs = (
        P("seq", "feat"),
        P("seq"),
        P("seq", "feat"),
        P("seq", None),
        P("seq", None),
        P("seq", "feat"),
    )
    out_specs = P("seq", "feat")
    return jax.shard_map(local, mesh=mesh, in_specs=in_specs, out_specs=out_specs, check_vma=False)
```

time: 974 us -> 601 us (0.62)
  matrix products: 261 us -> 14.6 us
  other arithmetic: 132 us -> 6.3 us
  local copies, waits for them, and re-layouts: 101 us -> 4.56 us
  Pallas kernels: 0 us -> 79.8 us
  waiting for transfers between devices: 440 us -> 458 us
    dot_general x17 -> x0, matrix products: 246 us -> none  [the longest x7 110 us: attend_block(): jnp.einsum('ngrk,knd->ngrd', probs.astype(jnp.bfloat16), value_heads, pre...]
    reduce_sum x7 -> x1, other arithmetic: 107 us -> 3.42 us  [local(): jnp.sum(segments[None, :] < segment_ids[:, None], axis=1, dtype=jnp.int32)]
    pallas_call x0 -> x3, Pallas kernels: none -> 79.8 us  [the longest x1 50.4 us: attend(): pl.pallas_call(attend_kernel, grid_spec=pltpu.PrefetchScalarGridSpec(num_...]
    all_gather x6 -> x4, waiting for transfers between devices: 264 us -> 336 us  [the longest x1 106 us: local(): kv = lax.all_gather(kv_local, 'seq', axis=0, tiled=True)]
    all_gather x1, waiting for transfers between devices: 113 us -> 60.1 us  [local(): lax.all_gather(attended, 'feat', axis=1, tiled=True)]
    reshape x9 -> x1, local copies, waits for them, and re-layouts: 25.4 us -> 0.09 us  [attend(): jnp.stack([starts[::ROWS], starts[ROWS - 1::ROWS]], axis=1).reshape(-1)]
    dynamic_slice x16 -> x1, local copies, waits for them, and re-layouts: 18.3 us -> 1.07 us  [local(): lax.dynamic_slice_in_dim(v_weight, kv_start, kv_width, 1)]
    cond x49 -> x0, local copies, waits for them, and re-layouts: 14.3 us -> none
  transfers between devices with their start and end apart: 8 -> 6, of which waited for: 7 -> 6; matrix products, arithmetic and copies ran while one was open for 48% -> 1% of each run, Pallas kernels for 0% -> 13%
where the time goes in v1:
time: 601 us; the launch traced here: 600 us
  waiting for transfers between devices  458 us (76%)
  Pallas kernels  79.8 us (13%)
  blocking collectives  22.3 us (4%)
  matrix products  14.6 us (2%)
  between operations  13.5 us (2%)
  other arithmetic  6.3 us (1%)
    all_gather x1, waiting for transfers between devices, local(): kv = lax.all_gather(kv_local, 'seq', axis=0, tiled=True)  106 us
    all_gather x1, waiting for transfers between devices, local(): q_panel = lax.all_gather(q_weight, 'seq', axis=0, tiled=True)  86.7 us
    all_gather x1, waiting for transfers between devices, local(): o_panel = lax.all_gather(o_weight, 'seq', axis=0, tiled=True)  73.1 us
    all_gather x1, waiting for transfers between devices, local(): kv_panel = lax.all_gather(kv_slice, 'seq', axis=0, tiled=True)  70.3 us
    all_gather x1, waiting for transfers between devices, local(): piece = lax.all_gather(tokens, 'feat', axis=1, tiled=True)  60.2 us
    all_gather x1, waiting for transfers between devices, local(): lax.all_gather(attended, 'feat', axis=1, tiled=True)  60.1 us
    pallas_call x1, Pallas kernels, attend(): pl.pallas_call(attend_kernel, grid_spec=pltpu.PrefetchScalarGridSpec(num_...  50.4 us
    pallas_call x2, Pallas kernels, project(): pl.pallas_call(functools.partial(project_kernel, rope_tiles), grid=(colum...  29.4 us
  transfers between devices with their start and end apart: 6, of which 6 were waited for; matrix products, arithmetic and copies ran while one was open for 1% of the time, Pallas kernels for 13%

profile of v1, /device:TPU:25, one launch (start us, length us, event | category | flops | bytes accessed | tf_op | source)
XLA Modules:
  0.0 599.7 jit_solution(4199136409458456953)
XLA Ops:
  6.5 0.0 all-gather.11.cloned.1.call-start
  6.5 1.1 constant_dynamic-slice_fusion
  7.6 0.8 pad_maximum_fusion
  8.4 0.0 all-gather.11.cloned.1.call-update
  8.5 0.0 all-gather.7.cloned.1.call-start
  8.5 0.7 all-gather.7.cloned.1.call-update
  9.2 0.0 all-gather.9.cloned.1.call-start
  9.3 0.7 all-gather.9.cloned.1.call-update
  10.0 0.0 all-gather.13.cloned.1.call-start
  10.0 1.9 fusion
  12.0 70.3 %all-gather.11.cloned.1.call-done.w_ref = bf16[4096,512]{1,0:T(8,128)(2,1)} async-done(((bf16[512,512]{1,0:T(8,128)(2,1)}), bf16[4096,512]{1,0:T(8,128)(2,1)}) %all-gather.11.cloned.1.call-update) | async-done | bytes 4194320 | tf_op jit(solution)/shard_map/all_gather | solution.py:196
  82.3 60.2 %all-gather.7.cloned.1.call-done.x_ref = bf16[1024,4096]{1,0:T(8,128)(2,1)} async-done(((bf16[1024,1024]{1,0:T(8,128)(2,1)}), bf16[1024,4096]{1,0:T(8,128)(2,1)}) %all-gather.7.cloned.1.call-update) | async-done | bytes 8388624 | tf_op jit(solution)/shard_map/all_gather | solution.py:195
  142.5 0.0 copy-start.2
  142.5 11.5 %shard_map.65 = bf16[1024,512]{1,0:T(8,128)(2,1)} custom-call(bf16[1024,4096]{1,0:T(8,128)(2,1)} %all-gather.7.cloned.1.call-done.x_ref, bf16[4096,512]{1,0:T(8,128)(2,1)} %all-gather.11.cloned.1.call-done.w_ref, f32[1024,128]{1,0:T(8,128)S(1)} %get-tuple-element.8.cos_ref, f32[1024,128]{1,0:T(8,128)S(1)} %get-tuple-element.5.sin_ref), custom_call_target="tpu_custom_call" | custom-call | flops 4294967296 | bytes 13631488 | tf_op jit(solution)/shard_map/pallas_call | solution.py:65
  154.0 0.0 all-gather.13.cloned.1.call-update
  154.0 0.0 all-gather.17.cloned.1.call-start
  154.0 0.5 all-gather.17.cloned.1.call-update
  154.6 0.0 all-gather.15.cloned.1.call-start
  154.6 0.0 copy-done.2
  154.6 22.3 %all_gather.21 = s32[8192]{0:T(1024)S(1)} all-gather(s32[1024]{0:T(1024)S(1)} %copy-done.2), channel_id=1, replica_groups=mesh['seq'=8,'feat'=4] {'seq'}, dimensions={0}, use_global_device_ids=true | all-gather | bytes 36864 | tf_op jit(solution)/shard_map/all_gather | solution.py:184
  177.0 3.4 convert_reduce_fusion
  180.4 0.1 slice.7
  180.5 0.1 slice.6
  180.6 0.1 copy.12
  180.7 0.1 reshape.39
  180.8 0.2 copy.13.start_ref
  181.0 0.1 pad_add_fusion.1.bounds
  181.1 86.7 %all-gather.9.cloned.1.call-done.w_ref = bf16[4096,1024]{1,0:T(8,128)(2,1)} async-done(((bf16[512,1024]{1,0:T(8,128)(2,1)}), bf16[4096,1024]{1,0:T(8,128)(2,1)}) %all-gather.9.cloned.1.call-update) | async-done | bytes 8388624 | tf_op jit(solution)/shard_map/all_gather | solution.py:198
  267.8 17.9 %shard_map.64.q_ref = bf16[1024,1024]{1,0:T(8,128)(2,1)S(1)} custom-call(bf16[1024,4096]{1,0:T(8,128)(2,1)} %all-gather.7.cloned.1.call-done.x_ref, bf16[4096,1024]{1,0:T(8,128)(2,1)} %all-gather.9.cloned.1.call-done.w_ref, f32[1024,128]{1,0:T(8,128)S(1)} %get-tuple-element.7.cos_ref, f32[1024,128]{1,0:T(8,128)S(1)} %get-tuple-element.6.sin_ref), custom_call_target="tpu_custom_call" | custom-call | flops 8589934592 | bytes 18874368 | tf_op jit(solution)/shard_map/pallas_call | solution.py:65
  285.8 0.0 copy-start
  285.8 1.3 copy-done
  287.1 105.9 %all-gather.13.cloned.1.call-done.k_ref.v_ref = bf16[8192,512]{1,0:T(8,128)(2,1)} async-done(((bf16[1024,512]{1,0:T(8,128)(2,1)}), bf16[8192,512]{1,0:T(8,128)(2,1)}) %all-gather.13.cloned.1.call-update) | async-done | bytes 8388624 | tf_op jit(solution)/shard_map/all_gather | solution.py:199
  393.0 0.0 copy-start.1
  393.0 1.6 copy-done.1
  394.6 50.4 %shard_map.66 = bf16[1024,1024]{1,0:T(8,128)(2,1)} custom-call(s32[9]{0:T(128)S(1)} %pad_add_fusion.1.bounds, bf16[1024,1024]{1,0:T(8,128)(2,1)S(1)} %copy-done.1, bf16[8192,512]{1,0:T(8,128)(2,1)} %all-gather.13.cloned.1.call-done.k_ref.v_ref, bf16[8192,512]{1,0:T(8,128)(2,1)} %all-gather.13.cloned.1.call-done.k_ref.v_ref, s32[1024,1]{1,0:T(8,128)S(1)} %copy.13.start_ref), custom_call_target="tpu_custom_call" | custom-call | flops 17179869184 | bytes 12582912 | tf_op jit(solution)/shard_map/pallas_call | solution.py:143
  445.0 0.0 all-gather.15.cloned.1.call-update
  445.0 73.1 %all-gather.17.cloned.1.call-done = bf16[4096,1024]{1,0:T(8,128)(2,1)} async-done(((bf16[512,1024]{1,0:T(8,128)(2,1)}), bf16[4096,1024]{1,0:T(8,128)(2,1)}) %all-gather.17.cloned.1.call-update) | async-done | bytes 8388624 | tf_op jit(solution)/shard_map/all_gather | solution.py:201
  518.2 60.1 %all-gather.15.cloned.1.call-done = bf16[1024,4096]{1,0:T(8,128)(2,1)} async-done(((bf16[1024,1024]{1,0:T(8,128)(2,1)}), bf16[1024,4096]{1,0:T(8,128)(2,1)}) %all-gather.15.cloned.1.call-update) | async-done | bytes 8388624 | tf_op jit(solution)/shard_map/all_gather | solution.py:204
  578.2 14.6 %convolution_convert_fusion = bf16[1024,1024]{1,0:T(8,128)(2,1)} fusion(bf16[1024,4096]{1,0:T(8,128)(2,1)} %all-gather.15.cloned.1.call-done, bf16[4096,1024]{1,0:T(8,128)(2,1)} %all-gather.17.cloned.1.call-done), kind=kOutput, calls=%fused_computation.1 | convolution fusion | flops 8590983168 | bytes 18874368 | tf_op jit(solution)/shard_map/dot_general | solution.py:203
  (3 shorter events, 0.0 us)
Async XLA Ops:
  6.5 75.8 %all-gather.11.cloned.1.call-start = ((), (), s32[]{:S(2)}) async-start(), calls=%async_computation.2 | async-start | bytes 4718592 | tf_op jit(solution)/shard_map/all_gather | solution.py:196
  8.5 134.0 %all-gather.7.cloned.1.call-start = ((), (), s32[]{:S(2)}) async-start(), calls=%async_computation | async-start | bytes 10485760 | tf_op jit(solution)/shard_map/all_gather | solution.py:195
  9.2 258.6 %all-gather.9.cloned.1.call-start = ((), (), s32[]{:S(2)}) async-start(), calls=%async_computation.1 | async-start | bytes 9437184 | tf_op jit(solution)/shard_map/all_gather | solution.py:198
  10.0 383.1 %all-gather.13.cloned.1.call-start = ((), (), s32[]{:S(2)}) async-start(), calls=%async_computation.3 | async-start | bytes 9437184 | tf_op jit(solution)/shard_map/all_gather | solution.py:199
  142.5 12.2 %copy-start.2 = (s32[1024]{0:T(1024)S(1)}, s32[1024]{0:T(1024)}, u32[]{:S(2)}) copy-start(s32[1024]{0:T(1024)} %param.7) | copy-start | bytes 12292
  154.0 364.2 %all-gather.17.cloned.1.call-start = ((), (), s32[]{:S(2)}) async-start(), calls=%async_computation.5 | async-start | bytes 9437184 | tf_op jit(solution)/shard_map/all_gather | solution.py:201
  154.6 423.6 %all-gather.15.cloned.1.call-start = ((), (), s32[]{:S(2)}) async-start(), calls=%async_computation.4 | async-start | bytes 10485760 | tf_op jit(solution)/shard_map/all_gather | solution.py:204
  285.8 1.3 copy-start
  393.0 1.6 copy-start.1
Sparse Core Ops, SparseCore 0:
  9.5 72.7 all-gather.10
  83.9 58.5 all-gather.6
  144.6 123.2 all-gather.8
  269.8 123.1 all-gather.12
  395.0 123.1 all-gather.16
  519.6 58.5 all-gather.14

commit v2 on v1

--- a/solution.py
+++ b/solution.py
@@ -27,14 +27,23 @@
     return jnp.cos(angle), jnp.sin(angle) * sign[None, :]
 
 
-def project_kernel(rope_tiles, x_ref, w_ref, cos_ref, sin_ref, o_ref):
+def project_kernel(rope_tiles, count, offsets, *refs):
+    x_refs = refs[:count]
+    w_ref, cos_ref, sin_ref, o_ref = refs[count:]
     column = pl.program_id(0)
-    rows = x_ref.shape[0]
+    rows, depth = x_refs[0].shape
 
     @pl.loop(0, rows // ROWS)
     def _(step):
         at = pl.ds(pl.multiple_of(step * ROWS, ROWS), ROWS)
-        raw = jnp.dot(x_ref[at, :], w_ref[...], preferred_element_type=jnp.float32)
+        raw = jnp.zeros((ROWS, w_ref.shape[1]), jnp.float32)
+        for number in range(count):
+            begin = pl.multiple_of(offsets[number], depth)
+            raw += jnp.dot(
+                x_refs[number][at, :],
+                w_ref[pl.ds(begin, depth), :],
+                preferred_element_type=jnp.float32,
+            )
 
         def turned():
             cosine = cos_ref[at, :]
@@ -52,34 +61,53 @@
         def plain():
             o_ref[at, :] = raw.astype(o_ref.dtype)
 
-        if rope_tiles is None:
+        if rope_tiles == "all":
             turned()
+        elif rope_tiles == "none":
+            plain()
         else:
             pl.when(column < rope_tiles)(turned)
             pl.when(column >= rope_tiles)(plain)
 
 
-def project(x, w, tables, tile, rope_tiles):
-    rows, depth = x.shape
+def project(pieces, offsets, w, tables, tile, rope_tiles):
+    rows, depth = pieces[0].shape
+    total = depth * len(pieces)
     columns = w.shape[1]
+    whole = lambda j, o: (0, 0)
     return pl.pallas_call(
-        functools.partial(project_kernel, rope_tiles),
-        grid=(columns // tile,),
+        functools.partial(project_kernel, rope_tiles, len(pieces)),
+        grid_spec=pltpu.PrefetchScalarGridSpec(
+            num_scalar_prefetch=1,
+            grid=(columns // tile,),
+            in_specs=[pl.BlockSpec((rows, depth), whole)] * len(pieces)
+            + [
+                pl.BlockSpec((total, tile), lambda j, o: (0, j)),
+                pl.BlockSpec((rows, HD), whole),
+                pl.BlockSpec((rows, HD), whole),
+            ],
+            out_specs=pl.BlockSpec((rows, tile), lambda j, o: (0, j)),
+        ),
         out_shape=jax.ShapeDtypeStruct((rows, columns), jnp.bfloat16),
-        in_specs=[
-            pl.BlockSpec((rows, depth), lambda j: (0, 0)),
-            pl.BlockSpec((depth, tile), lambda j: (0, j)),
-            pl.BlockSpec((rows, HD), lambda j: (0, 0)),
-            pl.BlockSpec((rows, HD), lambda j: (0, 0)),
-        ],
-        out_specs=pl.BlockSpec((rows, tile), lambda j: (0, j)),
         compiler_params=pltpu.CompilerParams(vmem_limit_bytes=VMEM_BYTES),
         cost_estimate=pl.CostEstimate(
-            flops=2 * rows * depth * columns,
-            bytes_accessed=2 * (rows * depth + depth * columns + rows * columns),
+            flops=2 * rows * total * columns,
+            bytes_accessed=2 * (rows * total + total * columns + rows * columns),
             transcendentals=0,
         ),
-    )(x, w, *tables)
+    )(offsets, *pieces, w, *tables)
+
+
+def exchange(block, axis):
+    count = lax.axis_size(axis)
+    pieces, numbers = [block], [0]
+    bit = count // 2
+    while bit:
+        pairs = [(index, index ^ bit) for index in range(count)]
+        pieces = pieces + [lax.ppermute(piece, axis, pairs) for piece in pieces]
+        numbers = numbers + [number ^ bit for number in numbers]
+        bit //= 2
+    return pieces, numbers
 
 
 def attend_kernel(bounds, q_ref, k_ref, v_ref, start_ref, o_ref, m_ref, acc_ref):
@@ -192,20 +220,21 @@
         ],
         axis=1,
     )
-    piece = lax.all_gather(tokens, "feat", axis=1, tiled=True)
+    pieces, numbers = exchange(tokens, "feat")
+    sources = jnp.stack([feat_index ^ number for number in numbers])
+    token_rows = sources * tokens.shape[1]
     kv_panel = lax.all_gather(kv_slice, "seq", axis=0, tiled=True)
-    kv_local = project(piece, kv_panel, (cosine, sine), kv_width, 1)
+    kv_local = project(pieces, token_rows, kv_panel, (cosine, sine), kv_width, 1)
     q_panel = lax.all_gather(q_weight, "seq", axis=0, tiled=True)
     kv = lax.all_gather(kv_local, "seq", axis=0, tiled=True)
-    queries = project(piece, q_panel, (cosine * factor, sine * factor), 256, None)
+    queries = project(
+        pieces, token_rows, q_panel, (cosine * factor, sine * factor), 256, "all"
+    )
     o_panel = lax.all_gather(o_weight, "seq", axis=0, tiled=True)
     attended = attend(queries, kv, starts, query_start, kv_heads)
-    result = jnp.dot(
-        lax.all_gather(attended, "feat", axis=1, tiled=True),
-        o_panel,
-        preferred_element_type=jnp.float32,
-    )
-    return result.astype(jnp.bfloat16)
+    mixed, _ = exchange(attended, "feat")
+    attended_rows = sources * attended.shape[1]
+    return project(mixed, attended_rows, o_panel, (cosine, sine), 256, "none")
 
 
 def solution(mesh):

time: 601 us -> 486 us (0.81)
  waiting for transfers between devices: 458 us -> 353 us
  matrix products: 14.6 us -> 0 us
  starting transfers between devices: 0.2 us -> 7.17 us
    all_gather x2 -> x0, waiting for transfers between devices: 120 us -> none  [the longest x1 60.2 us: local(): piece = lax.all_gather(tokens, 'feat', axis=1, tiled=True)]
    ppermute x0 -> x6, waiting for transfers between devices: none -> 91.8 us  [exchange(): pieces = pieces + [lax.ppermute(piece, axis, pairs) for piece in pieces]]
    all_gather x1, waiting for transfers between devices: 70.3 us -> 20.5 us  [local(): kv_panel = lax.all_gather(kv_slice, 'seq', axis=0, tiled=True)]
    all_gather x1, waiting for transfers between devices: 73.1 us -> 48 us  [local(): o_panel = lax.all_gather(o_weight, 'seq', axis=0, tiled=True)]
    pallas_call x1, Pallas kernels: 50.4 us -> 27.2 us  [attend(): pl.pallas_call(attend_kernel, grid_spec=pltpu.PrefetchScalarGridSpec(num_...]
    pallas_call x2 -> x3, Pallas kernels: 29.4 us -> 47.7 us  [project(): pl.pallas_call(functools.partial(project_kernel, rope_tiles, len(pieces))...]
    dot_general x1 -> x0, matrix products: 14.6 us -> none  [local(): jnp.dot(lax.all_gather(attended, 'feat', axis=1, tiled=True), o_panel, pr...]
    ppermute x0 -> x6, starting transfers between devices: none -> 7.05 us  [exchange(): pieces = pieces + [lax.ppermute(piece, axis, pairs) for piece in pieces]]
  transfers between devices with their start and end apart: 6 -> 10, of which waited for: 6 -> 7; matrix products, arithmetic and copies ran while one was open for 1% -> 1% of each run, Pallas kernels for 13% -> 12%
where the time goes in v2:
time: 486 us; the launch traced here: 482 us
  waiting for transfers between devices  353 us (73%)
  Pallas kernels  74.8 us (15%)
  blocking collectives  22.8 us (5%)
  between operations  13.2 us (3%)
  starting transfers between devices  7.17 us (1%)
  other arithmetic  6.38 us (1%)
    all_gather x1, waiting for transfers between devices, local(): kv = lax.all_gather(kv_local, 'seq', axis=0, tiled=True)  106 us
    ppermute x6, waiting for transfers between devices, exchange(): pieces = pieces + [lax.ppermute(piece, axis, pairs) for piece in pieces]  91.8 us
    all_gather x1, waiting for transfers between devices, local(): q_panel = lax.all_gather(q_weight, 'seq', axis=0, tiled=True)  85.8 us
    all_gather x1, waiting for transfers between devices, local(): o_panel = lax.all_gather(o_weight, 'seq', axis=0, tiled=True)  48 us
    pallas_call x3, Pallas kernels, project(): pl.pallas_call(functools.partial(project_kernel, rope_tiles, len(pieces))...  47.7 us
    pallas_call x1, Pallas kernels, attend(): pl.pallas_call(attend_kernel, grid_spec=pltpu.PrefetchScalarGridSpec(num_...  27.2 us
    all_gather x1, blocking collectives, local(): segments = lax.all_gather(segment_ids, 'seq', axis=0, tiled=True)  22.8 us
    all_gather x1, waiting for transfers between devices, local(): kv_panel = lax.all_gather(kv_slice, 'seq', axis=0, tiled=True)  20.5 us
  transfers between devices with their start and end apart: 10, of which 7 were waited for; matrix products, arithmetic and copies ran while one was open for 1% of the time, Pallas kernels for 12%

profile of v2, /device:TPU:25, one launch (start us, length us, event | category | flops | bytes accessed | tf_op | source)
XLA Modules:
  0.0 482.1 jit_solution(13506483887365156964)
XLA Ops:
  6.5 0.0 all-gather.7.cloned.1.call-start
  6.5 1.1 constant_dynamic-slice_fusion
  7.6 0.8 pad_maximum_fusion
  8.4 0.0 all-gather.7.cloned.1.call-update
  8.5 0.0 all-gather.5.cloned.1.call-start
  8.5 0.7 all-gather.5.cloned.1.call-update
  9.2 0.0 all-gather.9.cloned.1.call-start
  9.3 1.3 collective-permute-start
  10.6 1.0 collective-permute-start.1
  11.5 44.6 %collective-permute-done.refs_1_ = bf16[1024,1024]{1,0:T(8,128)(2,1)} collective-permute-done((bf16[1024,1024]{1,0:T(8,128)(2,1)}, bf16[1024,1024]{1,0:T(8,128)(2,1)}, u32[]{:S(2)}, u32[]{:S(2)}) %collective-permute-start) | collective-permute-done | bytes 2097184 | tf_op jit(solution)/shard_map/ppermute | solution.py:107
  56.1 1.5 collective-permute-start.2
  57.7 0.1 add_multiply_fusion.offsets
  57.8 1.9 fusion
  59.7 0.0 collective-permute-done.1.refs_2_
  59.7 2.1 collective-permute-done.2.refs_3_
  61.8 20.5 %all-gather.7.cloned.1.call-done.refs_4_ = bf16[4096,512]{1,0:T(8,128)(2,1)} async-done(((bf16[512,512]{1,0:T(8,128)(2,1)}), bf16[4096,512]{1,0:T(8,128)(2,1)}) %all-gather.7.cloned.1.call-update) | async-done | bytes 4194320 | tf_op jit(solution)/shard_map/all_gather | solution.py:226
  82.3 12.1 %shard_map.65 = bf16[1024,512]{1,0:T(8,128)(2,1)} custom-call(s32[4]{0:T(128)S(1)} %add_multiply_fusion.offsets, bf16[1024,1024]{1,0:T(8,128)(2,1)} %refs_0_.3, bf16[1024,1024]{1,0:T(8,128)(2,1)} %collective-permute-done.refs_1_, bf16[1024,1024]{1,0:T(8,128)(2,1)} %collective-permute-done.1.refs_2_, bf16[1024,1024]{1,0:T(8,128)(2,1)} %collective-permute-done.2.refs_3_, ...), custom_call_target="tpu_custom_call" | custom-call | flops 4294967296 | bytes 13631488 | tf_op jit(solution)/shard_map/pallas_call | solution.py:78
  94.4 0.0 copy-start.2
  94.4 0.0 all-gather.9.cloned.1.call-update
  94.4 0.0 all-gather.11.cloned.1.call-start
  94.5 0.5 all-gather.11.cloned.1.call-update
  95.0 0.1 copy-done.2
  95.1 22.8 %all_gather.15 = s32[8192]{0:T(1024)S(1)} all-gather(s32[1024]{0:T(1024)S(1)} %copy-done.2), channel_id=1, replica_groups=mesh['seq'=8,'feat'=4] {'seq'}, dimensions={0}, use_global_device_ids=true | all-gather | bytes 36864 | tf_op jit(solution)/shard_map/all_gather | solution.py:212
  117.9 3.4 convert_reduce_fusion
  121.4 0.1 slice.7
  121.5 0.1 slice.6
  121.6 0.1 copy.12
  121.7 0.1 reshape.39
  121.7 0.2 copy.13.start_ref
  122.0 0.1 pad_add_fusion.1.bounds
  122.1 85.8 %all-gather.5.cloned.1.call-done.refs_4_ = bf16[4096,1024]{1,0:T(8,128)(2,1)} async-done(((bf16[512,1024]{1,0:T(8,128)(2,1)}), bf16[4096,1024]{1,0:T(8,128)(2,1)}) %all-gather.5.cloned.1.call-update) | async-done | bytes 8388624 | tf_op jit(solution)/shard_map/all_gather | solution.py:228
  207.9 18.6 %shard_map.64.q_ref = bf16[1024,1024]{1,0:T(8,128)(2,1)S(1)} custom-call(s32[4]{0:T(128)S(1)} %add_multiply_fusion.offsets, bf16[1024,1024]{1,0:T(8,128)(2,1)} %refs_0_.3, bf16[1024,1024]{1,0:T(8,128)(2,1)} %collective-permute-done.refs_1_, bf16[1024,1024]{1,0:T(8,128)(2,1)} %collective-permute-done.1.refs_2_, ...), custom_call_target="tpu_custom_call" | custom-call | flops 8589934592 | bytes 18874368 | tf_op jit(solution)/shard_map/pallas_call | solution.py:78
  226.5 0.0 copy-start
  226.5 1.3 copy-done
  227.8 105.7 %all-gather.9.cloned.1.call-done.k_ref.v_ref = bf16[8192,512]{1,0:T(8,128)(2,1)} async-done(((bf16[1024,512]{1,0:T(8,128)(2,1)}), bf16[8192,512]{1,0:T(8,128)(2,1)}) %all-gather.9.cloned.1.call-update) | async-done | bytes 8388624 | tf_op jit(solution)/shard_map/all_gather | solution.py:229
  333.5 0.0 copy-start.1
  333.5 1.6 copy-done.1
  335.1 27.2 %shard_map.66.refs_0_ = bf16[1024,1024]{1,0:T(8,128)(2,1)} custom-call(s32[9]{0:T(128)S(1)} %pad_add_fusion.1.bounds, bf16[1024,1024]{1,0:T(8,128)(2,1)S(1)} %copy-done.1, bf16[8192,512]{1,0:T(8,128)(2,1)} %all-gather.9.cloned.1.call-done.k_ref.v_ref, bf16[8192,512]{1,0:T(8,128)(2,1)} %all-gather.9.cloned.1.call-done.k_ref.v_ref, s32[1024,1]{1,0:T(8,128)S(1)} %copy.13.start_ref), custom_call_target="tpu_custom_call" | custom-call | flops 17179869184 | bytes 12582912 | tf_op jit(solution)/shard_map/pallas_call | solution.py:171
  362.3 1.2 collective-permute-start.3
  363.5 0.7 collective-permute-start.4
  364.2 45.1 %collective-permute-done.3.refs_1_ = bf16[1024,1024]{1,0:T(8,128)(2,1)} collective-permute-done((bf16[1024,1024]{1,0:T(8,128)(2,1)}, bf16[1024,1024]{1,0:T(8,128)(2,1)}, u32[]{:S(2)}, u32[]{:S(2)}) %collective-permute-start.3) | collective-permute-done | bytes 2097184 | tf_op jit(solution)/shard_map/ppermute | solution.py:107
  409.3 1.3 collective-permute-start.5
  410.6 48.0 %all-gather.11.cloned.1.call-done.refs_4_ = bf16[4096,1024]{1,0:T(8,128)(2,1)} async-done(((bf16[512,1024]{1,0:T(8,128)(2,1)}), bf16[4096,1024]{1,0:T(8,128)(2,1)}) %all-gather.11.cloned.1.call-update) | async-done | bytes 8388624 | tf_op jit(solution)/shard_map/all_gather | solution.py:233
  458.7 0.0 collective-permute-done.4.refs_2_
  458.7 0.0 collective-permute-done.5.refs_3_
  458.7 16.9 %shard_map.67 = bf16[1024,1024]{1,0:T(8,128)(2,1)} custom-call(s32[4]{0:T(128)S(1)} %add_multiply_fusion.offsets, bf16[1024,1024]{1,0:T(8,128)(2,1)} %shard_map.66.refs_0_, bf16[1024,1024]{1,0:T(8,128)(2,1)} %collective-permute-done.3.refs_1_, bf16[1024,1024]{1,0:T(8,128)(2,1)} %collective-permute-done.4.refs_2_, ...), custom_call_target="tpu_custom_call" | custom-call | flops 8589934592 | bytes 18874368 | tf_op jit(solution)/shard_map/pallas_call | solution.py:78
  (3 shorter events, 0.0 us)
Async XLA Ops:
  6.5 75.8 %all-gather.7.cloned.1.call-start = ((), (), s32[]{:S(2)}) async-start(), calls=%async_computation.1 | async-start | bytes 4718592 | tf_op jit(solution)/shard_map/all_gather | solution.py:226
  8.5 199.4 %all-gather.5.cloned.1.call-start = ((), (), s32[]{:S(2)}) async-start(), calls=%async_computation | async-start | bytes 9437184 | tf_op jit(solution)/shard_map/all_gather | solution.py:228
  9.2 324.3 %all-gather.9.cloned.1.call-start = ((), (), s32[]{:S(2)}) async-start(), calls=%async_computation.2 | async-start | bytes 9437184 | tf_op jit(solution)/shard_map/all_gather | solution.py:229
  9.3 46.9 %collective-permute-start = (bf16[1024,1024]{1,0:T(8,128)(2,1)}, bf16[1024,1024]{1,0:T(8,128)(2,1)}, u32[]{:S(2)}, u32[]{:S(2)}) collective-permute-start(bf16[1024,1024]{1,0:T(8,128)(2,1)} %refs_0_.3), channel_id=1, source_target_pairs={{0,2},{1,3},{2,0},{3,1},{4,6},{5,7},{6,4},{7,5},{8,10},{9,11},{10,... | collective-permute-start | bytes 6291464 | tf_op jit(solution)/shard_map/ppermute | solution.py:107
  10.6 49.2 %collective-permute-start.1 = (bf16[1024,1024]{1,0:T(8,128)(2,1)}, bf16[1024,1024]{1,0:T(8,128)(2,1)}, u32[]{:S(2)}, u32[]{:S(2)}) collective-permute-start(bf16[1024,1024]{1,0:T(8,128)(2,1)} %refs_0_.3), channel_id=1, source_target_pairs={{0,1},{1,0},{2,3},{3,2},{4,5},{5,4},{6,7},{7,6},{8,9},{9,8},{10,11... | collective-permute-start | bytes 6291464 | tf_op jit(solution)/shard_map/ppermute | solution.py:107
  56.1 5.7 %collective-permute-start.2 = (bf16[1024,1024]{1,0:T(8,128)(2,1)}, bf16[1024,1024]{1,0:T(8,128)(2,1)}, u32[]{:S(2)}, u32[]{:S(2)}) collective-permute-start(bf16[1024,1024]{1,0:T(8,128)(2,1)} %collective-permute-done.refs_1_), channel_id=1, source_target_pairs={{0,1},{1,0},{2,3},{3,2},{4,5},{5,4},{6,7},{7,6},{8,9},{9,8},{10,11... | collective-permute-start | bytes 6291464 | tf_op jit(solution)/shard_map/ppermute | solution.py:107
  94.4 0.7 copy-start.2
  94.4 364.2 %all-gather.11.cloned.1.call-start = ((), (), s32[]{:S(2)}) async-start(), calls=%async_computation.3 | async-start | bytes 9437184 | tf_op jit(solution)/shard_map/all_gather | solution.py:233
  226.5 1.3 copy-start
  333.5 1.6 copy-start.1
  362.3 47.1 %collective-permute-start.3 = (bf16[1024,1024]{1,0:T(8,128)(2,1)}, bf16[1024,1024]{1,0:T(8,128)(2,1)}, u32[]{:S(2)}, u32[]{:S(2)}) collective-permute-start(bf16[1024,1024]{1,0:T(8,128)(2,1)} %shard_map.66.refs_0_), channel_id=1, source_target_pairs={{0,2},{1,3},{2,0},{3,1},{4,6},{5,7},{6,4},{7,5},{8,10},{9,11},{10,... | collective-permute-start | bytes 6291464 | tf_op jit(solution)/shard_map/ppermute | solution.py:107
  363.5 95.2 %collective-permute-start.4 = (bf16[1024,1024]{1,0:T(8,128)(2,1)}, bf16[1024,1024]{1,0:T(8,128)(2,1)}, u32[]{:S(2)}, u32[]{:S(2)}) collective-permute-start(bf16[1024,1024]{1,0:T(8,128)(2,1)} %shard_map.66.refs_0_), channel_id=1, source_target_pairs={{0,1},{1,0},{2,3},{3,2},{4,5},{5,4},{6,7},{7,6},{8,9},{9,8},{10,11... | collective-permute-start | bytes 6291464 | tf_op jit(solution)/shard_map/ppermute | solution.py:107
  409.3 49.3 %collective-permute-start.5 = (bf16[1024,1024]{1,0:T(8,128)(2,1)}, bf16[1024,1024]{1,0:T(8,128)(2,1)}, u32[]{:S(2)}, u32[]{:S(2)}) collective-permute-start(bf16[1024,1024]{1,0:T(8,128)(2,1)} %collective-permute-done.3.refs_1_), channel_id=1, source_target_pairs={{0,1},{1,0},{2,3},{3,2},{4,5},{5,4},{6,7},{7,6},{8,9},{9,8},{10,11... | collective-permute-start | bytes 6291464 | tf_op jit(solution)/shard_map/ppermute | solution.py:107
Sparse Core Ops, SparseCore 0:
  9.5 72.7 all-gather.6
  84.4 123.3 all-gather.4
  210.0 123.4 all-gather.8
  335.5 123.1 all-gather.10
